TPU v7x, 32 devices: a whole 2x2x4 slice. The times are simulated.
32 devices in a mesh: rep: 4 (over z), fsdp: 8 (over y, x, core).
Axes of the slice: x: 2, y: 2, z: 4, core: 2. Of those that a mesh axis runs over, the one named last changes fastest.
Arguments:
- grads: bfloat16 [4, 1024, 16384], P('rep', 'fsdp')
- moments: float32 [1024, 16384], P('fsdp', 'rep'), may hold values from 0.05 to 2
- factors: float32 [4, 8, 1024, 1024], P('rep', 'fsdp'), as said below
- roots: bfloat16 [4, 8, 1024, 1024], P('rep', 'fsdp'), as said below
- refresh: int32 [8], replicated, may hold values from 0 to 31, as said below
- owner: int32 [1, 16], replicated, may hold values from 0 to 3, as said below
Outputs:
- update: bfloat16 [1024, 16384], P('fsdp')
- new_moments: float32 [1024, 16384], P('fsdp', 'rep')
- new_factors: float32 [4, 8, 1024, 1024], P('rep', 'fsdp')
- new_roots: bfloat16 [4, 8, 1024, 1024], P('rep', 'fsdp')
Inputs may be any that keep to these rules, and one draw needn't show every extreme that they name: `refresh`: 8 distinct factor ids below 32; no two of them are held at the same fsdp index. `owner`: every band gives exactly 4 of its column blocks to each group. `factors`: each matrix is symmetric and positive definite. `roots`: each matrix is symmetric.
All inputs are finite; a program needn't handle non-finite values.
Results may differ from a plain program's by a relative error of at most 0.015.
Values may be sent and summed in bfloat16 or wider, within the bound.
A program may use at most 128 MiB of HBM per device.

v0:
```python
import functools

import jax
import jax.numpy as jnp
from jax import lax
from jax.experimental import pallas as pl
from jax.experimental.pallas import tpu as pltpu
from jax.sharding import PartitionSpec as P

NEWTON = 3


BETA_FACTOR = 0.9
BETA_MOMENT = 0.95
EPS_ADAM = 1e-08
EPS_NORM = 1e-06


def move_blocks(steps, source, target, order_ref, in_ref, out_ref, held, in_sem, out_sem):
    def arrive(i):
        return pltpu.make_async_copy(source(i, order_ref, in_ref), held.at[i], in_sem.at[i])

    def leave(i):
        return pltpu.make_async_copy(held.at[i], target(i, order_ref, out_ref), out_sem.at[i])

    def pass_on(i):
        arrive(i).wait()
        leave(i).start()

    pl.loop(0, steps)(lambda i: arrive(i).start())
    pl.loop(0, steps)(pass_on)
    pl.loop(0, steps)(lambda i: leave(i).wait())


def move_call(steps, source, target, order, array, held_shape, out_shape, name):
    return pl.pallas_call(
        functools.partial(move_blocks, steps, source, target),
        in_specs=[pl.BlockSpec(memory_space=pltpu.SMEM), pl.BlockSpec(memory_space=pl.ANY)],
        out_specs=pl.BlockSpec(memory_space=pl.ANY),
        out_shape=jax.ShapeDtypeStruct(out_shape, array.dtype),
        scratch_shapes=[
            pltpu.VMEM((steps,) + held_shape, array.dtype),
            pltpu.SemaphoreType.DMA((steps,)),
            pltpu.SemaphoreType.DMA((steps,)),
        ],
        compiler_params=pltpu.CompilerParams(vmem_limit_bytes=16 << 20),
        name=name,
    )(order, array)


def owner_order(rows, order, groups, per_group, pairs, sub_rows, block_size):
    def source(i, order_ref, in_ref):
        pair, group = i // groups, i % groups
        band, slot = pair // per_group, pair % per_group
        col = order_ref[band * groups * per_group + group * per_group + slot]
        return in_ref.at[
            pl.ds(pl.multiple_of(band * sub_rows, sub_rows), sub_rows),
            pl.ds(pl.multiple_of(col * block_size, block_size), block_size),
        ]

    def target(i, order_ref, out_ref):
        return out_ref.at[i // groups, i % groups]

    shape = (sub_rows, block_size)
    return move_call(
        pairs * groups, source, target, order, rows, shape, (pairs, groups) + shape, "owner_order"
    )


def natural_order(pieces, order, groups, per_group, pairs, sub_rows, block_size):
    half = block_size // 2

    def source(i, order_ref, in_ref):
        return in_ref.at[i // (2 * pairs), (i // 2) % pairs, i % 2]

    def target(i, order_ref, out_ref):
        group, pair, side = i // (2 * pairs), (i // 2) % pairs, i % 2
        band, slot = pair // per_group, pair % per_group
        col = order_ref[band * groups * per_group + group * per_group + slot]
        return out_ref.at[
            pl.ds(pl.multiple_of(band * sub_rows, sub_rows), sub_rows),
            pl.ds(pl.multiple_of(col * block_size + side * half, half), half),
        ]

    out_shape = (pairs // per_group * sub_rows, groups * per_group * block_size)
    return move_call(
        groups * pairs * 2, source, target, order, pieces, (sub_rows, half), out_shape, "natural_order"
    )


def exchange_kernel(
    groups, count, per_group, grads_hbm, moments_hbm, root_hbm, factor_hbm,
    upd, moments_out, factor_out, root_out,
    gp, right_buf, left_buf, pieces, block, moments, roots, product, upd_half, adam_out, adam_in,
    square_sums, factor, newton, norm,
    gp_sem, mom_sem, mom_out_sem, root_sem, factor_sem, factor_out_sem, root_out_sem, own_sem,
    right_send, right_recv, left_send, left_recv,
    piece_send, piece_recv, adam_send, adam_recv, root_send, root_recv, sq_send, sq_recv,
    upd_send, upd_recv, ag_right, ag_left, ag_recv,
):
    z, me = lax.axis_index("rep"), lax.axis_index("fsdp")
    pairs, _, sub_rows, size = gp.shape
    half = size // 2
    side, my_pair = me % 2, me // 2
    partner = me + 1 - 2 * side
    last = groups - 1

    def remote(src, dst, send, recv, **where):
        return pltpu.make_async_remote_copy(
            src_ref=src, dst_ref=dst, send_sem=send, recv_sem=recv,
            device_id=where, device_id_type=pl.DeviceIdType.MESH,
        )

    def load(k):
        return pltpu.make_async_copy(grads_hbm.at[k], gp.at[k], gp_sem.at[k])

    load(0).start()
    root_load = pltpu.make_async_copy(root_hbm, roots.at[side], root_sem)
    root_load.start()
    moments_load = pltpu.make_async_copy(moments_hbm, moments, mom_sem)
    moments_load.start()
    factor_load = pltpu.make_async_copy(factor_hbm, factor, factor_sem)
    factor_load.start()
    pl.loop(1, pairs)(lambda k: load(k).start())

    barrier = pltpu.get_barrier_semaphore()

    @pl.loop(1, count)
    def _(offset):
        pl.semaphore_signal(
            barrier, inc=1, device_id={"fsdp": (me + offset) % count},
            device_id_type=pl.DeviceIdType.MESH,
        )

    @pl.when(z > 0)
    def _():
        pl.semaphore_signal(
            barrier, inc=1, device_id={"rep": z - 1}, device_id_type=pl.DeviceIdType.MESH
        )

    @pl.when(z < last)
    def _():
        pl.semaphore_signal(
            barrier, inc=1, device_id={"rep": z + 1}, device_id_type=pl.DeviceIdType.MESH
        )

    pl.semaphore_wait(barrier, count - 1 + jnp.minimum(z, 1) + jnp.minimum(last - z, 1))

    def go_right(src, d, k):
        return remote(
            src, right_buf.at[k, d], right_send.at[k, d], right_recv.at[k, d],
            rep=jnp.minimum(z + 1, last),
        )

    def go_left(src, d, k):
        return remote(
            src, left_buf.at[k, d], left_send.at[k, d], left_recv.at[k, d],
            rep=jnp.maximum(z - 1, 0),
        )

    def send_raw(k):
        load(k).wait()
        for j in range(last):

            @pl.when(z == 0)
            def _():
                go_right(gp.at[k, last - j], last - j, k).start()

            @pl.when(z == last)
            def _():
                go_left(gp.at[k, j], j, k).start()

    def add_into(buf, k, d):
        buf[k, d] = (buf[k, d].astype(jnp.float32) + gp[k, d].astype(jnp.float32)).astype(buf.dtype)

    root_copy = remote(roots.at[side], roots.at[side], root_send, root_recv, fsdp=partner)

    def piece_copy(k, t):
        return remote(
            pieces.at[k], block.at[pl.ds(pl.multiple_of(me * sub_rows, sub_rows), sub_rows)],
            piece_send.at[k, t], piece_recv.at[me], fsdp=2 * k + t,
        )

    def adam_copy(k, t):
        return remote(
            adam_out.at[k], adam_in.at[me], adam_send.at[k, t], adam_recv.at[me], fsdp=2 * k + t
        )

    def reduce_slot(k):
        for j in range(last):
            far, near = last - j, j

            @pl.when((z > 0) & (z < far))
            def _():
                go_right(right_buf.at[k, far], far, k).wait_recv()
                add_into(right_buf, k, far)
                go_right(right_buf.at[k, far], far, k).start()

            @pl.when((z < last) & (z > near))
            def _():
                go_left(left_buf.at[k, near], near, k).wait_recv()
                add_into(left_buf, k, near)
                go_left(left_buf.at[k, near], near, k).start()

        @pl.when(z > 0)
        def _():
            go_right(right_buf.at[k, z], z, k).wait_recv()

        @pl.when(z < last)
        def _():
            go_left(left_buf.at[k, z], z, k).wait_recv()

        @pl.when(k == 0)
        def _():
            moments_load.wait()

        band, slot = k // per_group, k % per_group
        cols = pl.ds(pl.multiple_of(slot * size, size), size)

        def rows_step(i, total):
            part = pl.ds(pl.multiple_of(i * 16, 16), 16)
            rows = pl.ds(pl.multiple_of(band * sub_rows + i * 16, 16), 16)
            own = gp[k, z, part, :].astype(jnp.float32)
            from_left = right_buf[k, z, part, :].astype(jnp.float32)
            from_right = left_buf[k, z, part, :].astype(jnp.float32)
            own = own + jnp.where(z > 0, from_left, 0.0) + jnp.where(z < last, from_right, 0.0)
            gradient = own / groups
            moment = BETA_MOMENT * moments[rows, cols] + (1.0 - BETA_MOMENT) * gradient * gradient
            moments[rows, cols] = moment
            pieces[k, part, :] = gradient.astype(jnp.bfloat16)
            step = gradient / (jnp.sqrt(moment) + EPS_ADAM)
            return total + step * step

        total = lax.fori_loop(
            0, sub_rows // 16, rows_step, jnp.zeros((16, size), jnp.float32), unroll=2
        )
        adam_out[k] = jnp.full((8, 128), jnp.sum(total), jnp.float32)
        for t in range(2):

            @pl.when(me != 2 * k + t)
            def _():
                piece_copy(k, t).start()
                adam_copy(k, t).start()

        @pl.when(my_pair == k)
        def _():
            block[pl.ds(pl.multiple_of(me * sub_rows, sub_rows), sub_rows), :] = pieces[k]
            adam_in[me] = adam_out[k]

    tile = 256

    def own_slot(k):
        @pl.loop(0, count)
        def _(f):
            @pl.when(f != me)
            def _():
                remote(
                    pieces.at[k], block.at[pl.ds(pl.multiple_of(f * sub_rows, sub_rows), sub_rows)],
                    piece_send.at[k, 0], piece_recv.at[f], fsdp=partner,
                ).wait_recv()
                remote(
                    adam_out.at[k], adam_in.at[f], adam_send.at[k, 0], adam_recv.at[f], fsdp=partner
                ).wait_recv()

        root_copy_in = remote(
            roots.at[1 - side], roots.at[1 - side], root_send, root_recv, fsdp=partner
        )
        root_copy_in.wait_recv()
        half_cols = pl.ds(pl.multiple_of(side * half, half), half)

        def multiply(i, total):
            rows = pl.ds(pl.multiple_of(i * tile, tile), tile)
            mixed = jnp.dot(
                roots[0, rows, :], block[...], preferred_element_type=jnp.float32
            ).astype(jnp.bfloat16)
            result = jnp.dot(mixed, roots[1, :, half_cols], preferred_element_type=jnp.float32)
            product[rows, :] = result
            return total + jnp.sum(result * result)

        total = lax.fori_loop(0, size // tile, multiply, jnp.float32(0.0))
        square_sums[side] = jnp.full((8, 128), total, jnp.float32)
        remote(square_sums.at[side], square_sums.at[side], sq_send, sq_recv, fsdp=partner).start()
        remote(
            square_sums.at[1 - side], square_sums.at[1 - side], sq_send, sq_recv, fsdp=partner
        ).wait_recv()
        product_sq = square_sums[0] + square_sums[1]
        adam_sq = jnp.sum(adam_in[...], axis=0)
        scale = (jnp.sqrt(adam_sq) * lax.rsqrt(product_sq + EPS_NORM))[:1, :1]

        @pl.loop(0, count)
        def _(step):
            f = (me + step) % count
            rows = pl.ds(pl.multiple_of(f * sub_rows, sub_rows), sub_rows)
            upd_half[rows, :] = (product[rows, :] * scale).astype(jnp.bfloat16)

            @pl.when(f != me)
            def _():
                remote(
                    upd_half.at[rows], upd.at[z, k, side], upd_send.at[f], upd_recv.at[k, side],
                    fsdp=f,
                ).start()

            @pl.when(f == me)
            def _():
                pltpu.make_async_copy(upd_half.at[rows], upd.at[z, k, side], own_sem).start()

    def pass_right(s, k):
        return remote(
            upd.at[s, k], upd.at[s, k], ag_right.at[s, k], ag_recv.at[s, k],
            rep=jnp.minimum(z + 1, last),
        )

    def pass_left(s, k):
        return remote(
            upd.at[s, k], upd.at[s, k], ag_left.at[s, k], ag_recv.at[s, k],
            rep=jnp.maximum(z - 1, 0),
        )

    def tiles(body):
        pl.loop(0, size // tile)(lambda i: body(pl.ds(pl.multiple_of(i * tile, tile), tile)))

    def times(dst, lhs, rhs):
        @tiles
        def _(rows):
            newton[dst, rows, :] = jnp.dot(
                newton[lhs, rows, :], newton[rhs], preferred_element_type=jnp.float32
            ).astype(jnp.bfloat16)

    def step_rows(rows, state):
        shape = (tile, size)
        on_diagonal = lax.broadcasted_iota(jnp.int32, shape, 0) + rows.start == (
            lax.broadcasted_iota(jnp.int32, shape, 1)
        )
        return ((jnp.where(on_diagonal, 5.0, 0.0) - state.astype(jnp.float32)) * 0.25).astype(
            jnp.bfloat16
        )

    def step_from(state):
        @tiles
        def _(rows):
            newton[1, rows, :] = step_rows(rows, newton[state, rows, :])

    def gram():
        factor_load.wait()

        @pl.when(side == 0)
        def _():
            @tiles
            def _(rows):
                newton[3, rows, :] = block[rows, :]

        @pl.when(side == 1)
        def _():
            @tiles
            def _(rows):
                newton[3, :, rows] = block[rows, :].T

        def add_gram(i, total):
            rows = pl.ds(pl.multiple_of(i * tile, tile), tile)
            product_rows = lax.dot_general(
                newton[3, rows, :], newton[3], (((1,), (1,)), ((), ())),
                preferred_element_type=jnp.float32,
            )
            new = BETA_FACTOR * factor[rows, :] + (1.0 - BETA_FACTOR) * product_rows
            factor[rows, :] = new
            return total + jnp.sum(new * new)

        total = lax.fori_loop(0, size // tile, add_gram, jnp.float32(0.0))
        norm[...] = jnp.sqrt(jnp.full((8, 128), total, jnp.float32))
        pltpu.make_async_copy(factor, factor_out, factor_out_sem).start()

    def seed():
        z_norm = norm[...]
        first = lax.rsqrt(jnp.sqrt(z_norm))[:1, :1].astype(jnp.bfloat16).astype(jnp.float32)

        @tiles
        def _(rows):
            state = (factor[rows, :] / z_norm[:1, :1]).astype(jnp.bfloat16)
            newton[0, rows, :] = state
            step_mat = step_rows(rows, state)
            newton[1, rows, :] = step_mat
            newton[4, rows, :] = (first * step_mat.astype(jnp.float32)).astype(jnp.bfloat16)

    def first_state():
        times(2, 3, 0)
        step_from(2)

    def second_state():
        times(3, 4, 2)
        step_from(3)

    def finish():
        times(2, 0, 1)
        pltpu.make_async_copy(newton.at[2], root_out, root_out_sem).start()

    stages = [
        gram, seed, lambda: times(2, 1, 1), lambda: times(3, 2, 2), first_state,
        lambda: times(0, 4, 1), lambda: times(3, 1, 1), lambda: times(4, 3, 3), second_state,
        finish,
    ]

    def gather_slot(k, fill=lambda j: None):
        for t in range(2):

            @pl.when(me == 2 * k + t)
            def _():
                pltpu.make_async_copy(
                    upd_half.at[pl.ds(pl.multiple_of(me * sub_rows, sub_rows), sub_rows)],
                    upd.at[z, k, t], own_sem,
                ).wait()

            @pl.when(me != 2 * k + t)
            def _():
                remote(
                    upd_half.at[pl.ds(0, sub_rows)], upd.at[z, k, t], upd_send.at[0],
                    upd_recv.at[k, t], fsdp=partner,
                ).wait_recv()

        @pl.when(z < last)
        def _():
            pass_right(z, k).start()

        @pl.when(z > 0)
        def _():
            pass_left(z, k).start()

        for j in range(1, groups):
            fill(j)

            @pl.when(z - j >= 0)
            def _():
                s = z - j
                pass_right(s, k).wait_recv()

                @pl.when(z < last)
                def _():
                    pass_right(s, k).start()

            @pl.when(z + j <= last)
            def _():
                s = z + j
                pass_left(s, k).wait_recv()

                @pl.when(z > 0)
                def _():
                    pass_left(s, k).start()

    send_raw(0)
    root_load.wait()
    root_copy.start()
    send_raw(1)

    @pl.loop(0, pairs)
    def _(t):
        @pl.when(t + 2 < pairs)
        def _():
            send_raw(t + 2)

        reduce_slot(t)

        @pl.when(my_pair == t - 1)
        def _():
            own_slot(t - 1)

        @pl.when(t >= 2)
        def _():
            gather_slot(t - 2)

    pltpu.make_async_copy(moments, moments_out, mom_out_sem).start()

    @pl.when(my_pair == pairs - 1)
    def _():
        own_slot(pairs - 1)

    def fill_early(j):
        if j < 3:
            stages[j - 1]()

    def fill_late(j):
        for stage in stages[j + 1:j + 2] if j < groups - 1 else stages[j + 1:]:
            stage()

    gather_slot(pairs - 2, fill_early)
    gather_slot(pairs - 1, fill_late)
    root_copy.wait_send()
    remote(square_sums.at[side], square_sums.at[side], sq_send, sq_recv, fsdp=partner).wait_send()
    pltpu.make_async_copy(moments, moments_out, mom_out_sem).wait()
    pltpu.make_async_copy(factor, factor_out, factor_out_sem).wait()
    pltpu.make_async_copy(newton.at[2], root_out, root_out_sem).wait()

    @pl.loop(0, count)
    def _(f):
        @pl.when(f != me)
        def _():
            rows = pl.ds(pl.multiple_of(f * sub_rows, sub_rows), sub_rows)
            remote(
                upd_half.at[rows], upd.at[z, my_pair, side], upd_send.at[f],
                upd_recv.at[my_pair, side], fsdp=f,
            ).wait_send()

    @pl.loop(0, pairs)
    def _(k):
        for t in range(2):

            @pl.when(me != 2 * k + t)
            def _():
                piece_copy(k, t).wait_send()
                adam_copy(k, t).wait_send()

        for d in range(groups):

            @pl.when(z < d)
            def _():
                go_right(right_buf.at[k, d], d, k).wait_send()

            @pl.when(z > d)
            def _():
                go_left(left_buf.at[k, d], d, k).wait_send()

            @pl.when((d <= z) & (z < last))
            def _():
                pass_right(d, k).wait_send()

            @pl.when((d >= z) & (z > 0))
            def _():
                pass_left(d, k).wait_send()


def exchange(ordered, moments, root, factor, per_group, count):
    pairs, groups, sub_rows, size = ordered.shape
    half = size // 2
    low, wide = jnp.bfloat16, jnp.float32
    dma = pltpu.SemaphoreType.DMA
    anywhere = pl.BlockSpec(memory_space=pl.ANY)
    return pl.pallas_call(
        functools.partial(exchange_kernel, groups, count, per_group),
        in_specs=[anywhere] * 4,
        out_specs=[anywhere] * 4,
        out_shape=[
            jax.ShapeDtypeStruct((groups, pairs, 2, sub_rows, half), low),
            jax.ShapeDtypeStruct(moments.shape, wide),
            jax.ShapeDtypeStruct((size, size), wide),
            jax.ShapeDtypeStruct((size, size), low),
        ],
        scratch_shapes=[
            pltpu.VMEM((pairs, groups, sub_rows, size), low),
            pltpu.VMEM((pairs, groups, sub_rows, size), low),
            pltpu.VMEM((pairs, groups, sub_rows, size), low),
            pltpu.VMEM((pairs, sub_rows, size), low),
            pltpu.VMEM((size, size), low),
            pltpu.VMEM(moments.shape, wide),
            pltpu.VMEM((2, size, size), low),
            pltpu.VMEM((size, half), wide),
            pltpu.VMEM((size, half), low),
            pltpu.VMEM((pairs, 8, 128), wide),
            pltpu.VMEM((count, 8, 128), wide),
            pltpu.VMEM((2, 8, 128), wide),
            pltpu.VMEM((size, size), wide),
            pltpu.VMEM((5, size, size), low),
            pltpu.VMEM((8, 128), wide),
            dma((pairs,)), dma, dma, dma, dma, dma, dma, dma,
            dma((pairs, groups)), dma((pairs, groups)), dma((pairs, groups)), dma((pairs, groups)),
            dma((pairs, 2)), dma((count,)), dma((pairs, 2)), dma((count,)), dma, dma, dma, dma,
            dma((count,)), dma((pairs, 2)), dma((groups, pairs)), dma((groups, pairs)),
            dma((groups, pairs)),
        ],
        compiler_params=pltpu.CompilerParams(
            collective_id=0, has_side_effects=True, vmem_limit_bytes=56 << 20
        ),
        name="exchange",
    )(ordered, moments, root, factor)


def local(grads, moments, factors, roots, refresh, owner):
    block_size = factors.shape[2]
    height = grads.shape[1]
    width_all = grads.shape[2]
    band_span = block_size // height
    groups = lax.axis_size("rep")
    columns = width_all // block_size
    per_group = columns // groups
    fsdp_count = lax.axis_size("fsdp")
    sub_rows = block_size // fsdp_count
    band_count = height // sub_rows
    half_cols = block_size // 2
    group_index = lax.axis_index("rep")
    fsdp_index = lax.axis_index("fsdp")
    band_index = fsdp_index // band_span
    local_index = fsdp_index % band_span
    side_index = local_index % 2
    slot_index = local_index // 2
    col_range = jnp.arange(columns, dtype=jnp.int32)
    col_order = jnp.argsort(owner * columns + col_range[None, :], axis=1)
    pairs = band_count * per_group
    order = col_order.reshape(-1).astype(jnp.int32)
    ordered = owner_order(grads[0], order, groups, per_group, pairs, sub_rows, block_size)
    own_root = roots[0, 0]
    gathered, new_moments, new_factor, fresh_root = exchange(
        ordered, moments, own_root, factors[0, 0], per_group, fsdp_count
    )
    update = natural_order(gathered, order, groups, per_group, pairs, sub_rows, block_size)
    pair_ids = refresh // 2
    listed_band = pair_ids // columns
    listed_col = pair_ids % columns
    listed_rows = jnp.take(owner, listed_band, axis=0)
    listed_group = jnp.take_along_axis(listed_rows, listed_col[:, None], axis=1)[:, 0]
    listed_rank = jnp.sum(
        (
            (listed_rows == listed_group[:, None]) & (col_range[None, :] < listed_col[:, None])
        ).astype(jnp.int32),
        axis=1,
    )
    listed_fsdp = listed_band * band_span + 2 * listed_rank + refresh % 2
    chosen = jnp.any((listed_group == group_index) & (listed_fsdp == fsdp_index))
    new_root = jnp.where(chosen, fresh_root, own_root)
    return (update, new_moments, new_factor[None, None], new_root[None, None])


def solution(mesh):
    placed = (
        P("rep", "fsdp", None),
        P("fsdp", "rep"),
        P("rep", "fsdp", None, None),
        P("rep", "fsdp", None, None),
        P(),
        P(),
    )
    return jax.shard_map(
        local,
        mesh=mesh,
        in_specs=placed,
        out_specs=(
            P("fsdp", None),
            P("fsdp", "rep"),
            P("rep", "fsdp", None, None),
            P("rep", "fsdp", None, None),
        ),
        check_vma=False,
    )
```

profile of v0, /device:TPU:6, one launch (start us, length us, event | category | flops | bytes accessed | tf_op | source)
XLA Modules:
  0.0 221.5 jit_solution(178913291107297039)
XLA Ops:
  0.6 0.7 iota_add_fusion
  1.3 0.1 copy.14
  1.4 0.7 sort.17
  2.1 0.1 reduce.order_ref
  2.2 0.0 copy-start.1
  2.2 2.2 copy-done.1
  4.4 2.1 owner_order.1.grads_hbm
  6.5 0.0 copy-start
  6.6 2.0 copy-done
  8.6 192.7 %exchange.1 = (bf16[4,4,2,128,512]{4,3,2,1,0:T(8,128)(2,1)}, f32[128,4096]{1,0:T(8,128)}, f32[1024,1024]{1,0:T(8,128)}, bf16[1024,1024]{1,0:T(8,128)(2,1)}) custom-call(bf16[4,4,128,1024]{3,2,1,0:T(8,128)(2,1)} %copy-done, f32[128,4096]{1,0:T(8,128)} %moments_hbm.1, bf16[1024,1024]{1,0:T(8,128)(2,1)} %bitcast.15, f32[1024,1024]{1,0:T(8,128)} %bitcast.16), custom_call_target="tpu_custom_call" | custom-call | tf_op jit(solution)/shard_map/exchange/pallas_call | solution.py:535
  201.3 0.0 copy-start.2
  201.3 2.2 copy-done.2
  203.5 0.0 copy-start.7
  203.5 0.0 copy-start.6
  203.5 0.0 copy-start.3
  203.5 9.1 %natural_order.1 = bf16[128,16384]{1,0:T(8,128)(2,1)} custom-call(s32[16]{0:T(128)S(1)} %reduce.order_ref, bf16[4,4,2,128,512]{4,3,2,1,0:T(8,128)(2,1)S(1)} %copy-done.2), custom_call_target="tpu_custom_call" | custom-call | tf_op jit(solution)/shard_map/natural_order/pallas_call | solution.py:36
  212.6 0.0 copy-done.7
  212.6 0.0 copy-done.6
  212.6 0.1 broadcast_select_fusion
  212.8 0.6 gather_fusion
  213.4 0.2 convert_reduce_fusion
  213.6 0.7 and_reduce_fusion
  214.2 0.0 copy-done.3
  214.2 0.0 copy-start.5
  214.2 2.3 %select_bitcast_fusion = bf16[1,1,1024,1024]{3,2,1,0:T(8,128)(2,1)} fusion(bf16[1024,1024]{1,0:T(8,128)(2,1)} %get-tuple-element.13, pred[]{:T(512)} %and_reduce_fusion, bf16[1,1,1024,1024]{3,2,1,0:T(8,128)(2,1)S(1)} %copy-done.3), kind=kLoop, calls=%fused_computation.1 | loop fusion | flops 1048576 | bytes 6291457 | tf_op jit(solution)/shard_map/broadcast_in_dim | solution.py:616
  216.6 0.0 copy-done.5
  216.6 0.0 copy-start.4
  216.6 1.3 copy.17
  217.9 1.6 copy-done.4
  219.5 2.0 copy.18
  (7 shorter events, 0.1 us)
Async XLA Ops:
  2.2 2.2 copy-start.1
  6.5 2.0 copy-start
  201.3 2.2 copy-start.2
  203.5 9.1 %copy-start.7 = (s32[8]{0:T(128)S(1)}, s32[8]{0:T(128)}, u32[]{:S(2)}) copy-start(s32[8]{0:T(128)} %param.10) | copy-start | bytes 100
  203.5 9.2 %copy-start.6 = (s32[1,16]{1,0:T(1,128)S(1)}, s32[1,16]{1,0:T(1,128)}, u32[]{:S(2)}) copy-start(s32[1,16]{1,0:T(1,128)} %param.11) | copy-start | bytes 196
  203.5 10.8 %copy-start.3 = (bf16[1,1,1024,1024]{3,2,1,0:T(8,128)(2,1)S(1)}, bf16[1,1,1024,1024]{3,2,1,0:T(8,128)(2,1)}, u32[]{:S(2)}) copy-start(bf16[1,1,1024,1024]{3,2,1,0:T(8,128)(2,1)} %param.9) | copy-start | bytes 6291460
  214.2 2.3 %copy-start.5 = (f32[128,4096]{1,0:T(8,128)S(1)}, f32[128,4096]{1,0:T(8,128)}, u32[]{:S(2)}) copy-start(f32[128,4096]{1,0:T(8,128)} %get-tuple-element.24) | copy-start | bytes 6291460
  216.6 2.9 %copy-start.4 = (f32[1024,1024]{1,0:T(8,128)S(1)}, f32[1024,1024]{1,0:T(8,128)}, u32[]{:S(2)}) copy-start(f32[1024,1024]{1,0:T(8,128)} %get-tuple-element.12) | copy-start | bytes 12582916
where the time goes:
time: 222 us
  Pallas kernels  204 us (92%)
  local copies, waits for them, and re-layouts  12.1 us (5%)
  other arithmetic  4.79 us (2%)
    pallas_call x1, Pallas kernels, exchange(): pl.pallas_call(functools.partial(exchange_kernel, groups, count, per_grou...  193 us
    unnamed x19, local copies, waits for them, and re-layouts  11.4 us
    pallas_call x2, Pallas kernels, move_call(): pl.pallas_call(functools.partial(move_blocks, steps, source, target), in_...  11.2 us

commit v1 on v0

--- a/solution.py
+++ b/solution.py
@@ -399,7 +399,7 @@
         finish,
     ]
 
-    def gather_slot(k, fill=lambda j: None):
+    def gather_start(k):
         for t in range(2):
 
             @pl.when(me == 2 * k + t)
@@ -424,26 +424,24 @@
         def _():
             pass_left(z, k).start()
 
-        for j in range(1, groups):
-            fill(j)
-
-            @pl.when(z - j >= 0)
-            def _():
-                s = z - j
-                pass_right(s, k).wait_recv()
-
-                @pl.when(z < last)
-                def _():
-                    pass_right(s, k).start()
-
-            @pl.when(z + j <= last)
-            def _():
-                s = z + j
-                pass_left(s, k).wait_recv()
-
-                @pl.when(z > 0)
-                def _():
-                    pass_left(s, k).start()
+    def gather_hop(k, j):
+        @pl.when(z - j >= 0)
+        def _():
+            s = z - j
+            pass_right(s, k).wait_recv()
+
+            @pl.when(z < last)
+            def _():
+                pass_right(s, k).start()
+
+        @pl.when(z + j <= last)
+        def _():
+            s = z + j
+            pass_left(s, k).wait_recv()
+
+            @pl.when(z > 0)
+            def _():
+                pass_left(s, k).start()
 
     send_raw(0)
     root_load.wait()
@@ -464,7 +462,13 @@
 
         @pl.when(t >= 2)
         def _():
-            gather_slot(t - 2)
+            gather_start(t - 2)
+
+        for j in range(1, groups):
+
+            @pl.when(t >= 2 + j)
+            def _():
+                gather_hop(t - 2 - j, j)
 
     pltpu.make_async_copy(moments, moments_out, mom_out_sem).start()
 
@@ -472,16 +476,22 @@
     def _():
         own_slot(pairs - 1)
 
-    def fill_early(j):
-        if j < 3:
-            stages[j - 1]()
-
-    def fill_late(j):
-        for stage in stages[j + 1:j + 2] if j < groups - 1 else stages[j + 1:]:
+    def hops(turn):
+        for j in range(groups - 1, 0, -1):
+            if 0 <= turn - j < pairs:
+                gather_hop(turn - j, j)
+
+    gather_start(pairs - 2)
+    hops(pairs - 2)
+    gather_start(pairs - 1)
+    stages[0]()
+    hops(pairs - 1)
+    stages[1]()
+    for turn in range(groups - 1):
+        done = turn + 2
+        for stage in stages[done:done + 1] if turn < groups - 2 else stages[done:]:
             stage()
-
-    gather_slot(pairs - 2, fill_early)
-    gather_slot(pairs - 1, fill_late)
+        hops(pairs + turn)
     root_copy.wait_send()
     remote(square_sums.at[side], square_sums.at[side], sq_send, sq_recv, fsdp=partner).wait_send()
     pltpu.make_async_copy(moments, moments_out, mom_out_sem).wait()

time: 222 us -> 227 us (1.023)
  Pallas kernels: 204 us -> 209 us
    pallas_call x1, Pallas kernels: 193 us -> 198 us  [exchange(): pl.pallas_call(functools.partial(exchange_kernel, groups, count, per_grou...]
where the time goes in v1:
time: 227 us
  Pallas kernels  209 us (92%)
  local copies, waits for them, and re-layouts  12.1 us (5%)
  other arithmetic  4.79 us (2%)
    pallas_call x1, Pallas kernels, exchange(): pl.pallas_call(functools.partial(exchange_kernel, groups, count, per_grou...  198 us
    unnamed x19, local copies, waits for them, and re-layouts  11.4 us
    pallas_call x2, Pallas kernels, move_call(): pl.pallas_call(functools.partial(move_blocks, steps, source, target), in_...  11.2 us

profile of v1, /device:TPU:6, one launch (start us, length us, event | category | flops | bytes accessed | tf_op | source)
XLA Modules:
  0.0 226.7 jit_solution(2723222746278080170)
XLA Ops:
  0.6 0.7 iota_add_fusion
  1.3 0.1 copy.14
  1.4 0.7 sort.17
  2.1 0.1 reduce.order_ref
  2.2 0.0 copy-start.1
  2.2 2.2 copy-done.1
  4.4 2.1 owner_order.1.grads_hbm
  6.5 0.0 copy-start
  6.6 2.0 copy-done
  8.6 197.8 %exchange.1 = (bf16[4,4,2,128,512]{4,3,2,1,0:T(8,128)(2,1)}, f32[128,4096]{1,0:T(8,128)}, f32[1024,1024]{1,0:T(8,128)}, bf16[1024,1024]{1,0:T(8,128)(2,1)}) custom-call(bf16[4,4,128,1024]{3,2,1,0:T(8,128)(2,1)} %copy-done, f32[128,4096]{1,0:T(8,128)} %moments_hbm.1, bf16[1024,1024]{1,0:T(8,128)(2,1)} %bitcast.15, f32[1024,1024]{1,0:T(8,128)} %bitcast.16), custom_call_target="tpu_custom_call" | custom-call | tf_op jit(solution)/shard_map/exchange/pallas_call | solution.py:545
  206.4 0.0 copy-start.2
  206.4 2.2 copy-done.2
  208.6 0.0 copy-start.7
  208.6 0.0 copy-start.6
  208.6 0.0 copy-start.3
  208.6 9.1 %natural_order.1 = bf16[128,16384]{1,0:T(8,128)(2,1)} custom-call(s32[16]{0:T(128)S(1)} %reduce.order_ref, bf16[4,4,2,128,512]{4,3,2,1,0:T(8,128)(2,1)S(1)} %copy-done.2), custom_call_target="tpu_custom_call" | custom-call | tf_op jit(solution)/shard_map/natural_order/pallas_call | solution.py:36
  217.7 0.0 copy-done.7
  217.8 0.0 copy-done.6
  217.8 0.1 broadcast_select_fusion
  217.9 0.6 gather_fusion
  218.5 0.2 convert_reduce_fusion
  218.7 0.7 and_reduce_fusion
  219.4 0.0 copy-done.3
  219.4 0.0 copy-start.5
  219.4 2.3 %select_bitcast_fusion = bf16[1,1,1024,1024]{3,2,1,0:T(8,128)(2,1)} fusion(bf16[1024,1024]{1,0:T(8,128)(2,1)} %get-tuple-element.13, pred[]{:T(512)} %and_reduce_fusion, bf16[1,1,1024,1024]{3,2,1,0:T(8,128)(2,1)S(1)} %copy-done.3), kind=kLoop, calls=%fused_computation.1 | loop fusion | flops 1048576 | bytes 6291457 | tf_op jit(solution)/shard_map/broadcast_in_dim | solution.py:626
  221.7 0.0 copy-done.5
  221.7 0.0 copy-start.4
  221.7 1.3 copy.17
  223.0 1.6 copy-done.4
  224.7 2.0 copy.18
  (7 shorter events, 0.1 us)
Async XLA Ops:
  2.2 2.2 copy-start.1
  6.5 2.0 copy-start
  206.4 2.2 copy-start.2
  208.6 9.1 %copy-start.7 = (s32[8]{0:T(128)S(1)}, s32[8]{0:T(128)}, u32[]{:S(2)}) copy-start(s32[8]{0:T(128)} %param.10) | copy-start | bytes 100
  208.6 9.2 %copy-start.6 = (s32[1,16]{1,0:T(1,128)S(1)}, s32[1,16]{1,0:T(1,128)}, u32[]{:S(2)}) copy-start(s32[1,16]{1,0:T(1,128)} %param.11) | copy-start | bytes 196
  208.6 10.8 %copy-start.3 = (bf16[1,1,1024,1024]{3,2,1,0:T(8,128)(2,1)S(1)}, bf16[1,1,1024,1024]{3,2,1,0:T(8,128)(2,1)}, u32[]{:S(2)}) copy-start(bf16[1,1,1024,1024]{3,2,1,0:T(8,128)(2,1)} %param.9) | copy-start | bytes 6291460
  219.4 2.3 %copy-start.5 = (f32[128,4096]{1,0:T(8,128)S(1)}, f32[128,4096]{1,0:T(8,128)}, u32[]{:S(2)}) copy-start(f32[128,4096]{1,0:T(8,128)} %get-tuple-element.24) | copy-start | bytes 6291460
  221.7 2.9 %copy-start.4 = (f32[1024,1024]{1,0:T(8,128)S(1)}, f32[1024,1024]{1,0:T(8,128)}, u32[]{:S(2)}) copy-start(f32[1024,1024]{1,0:T(8,128)} %get-tuple-element.12) | copy-start | bytes 12582916
